TPU v7x, 256 devices: a whole 4x4x8 slice. The times are simulated.
256 devices in a mesh: row: 32 (over z, x), col: 8 (over y, core).
Axes of the slice: x: 4, y: 4, z: 8, core: 2. Of those that a mesh axis runs over, the one named last changes fastest.
Arguments:
- panel: float32 [128, 524288], P('col', 'row'), may hold values from -6 to 6
- signs: int32 [524288], P('row'), may hold values from -1 to 1, as said below
- offsets: int32 [32768], P('row'), may hold values from 0 to 16383
- owners: int32 [32768, 1], P('row'), may hold values from 0 to 31; in each aligned block of 1024 rows (0 to 1023, 1024 to 2047, ...) at most 64 rows name the same one
Outputs:
- grams: float32 [32, 128, 128], P('row', 'col')
Inputs may be any that keep to these rules, and one draw needn't show every extreme that they name: `signs`: each entry is +1 or -1. `owners`: in each aligned block of 1024 samples (the list of one source), no owner is named more than 64 times, a bound that some block reaches; every owner is named somewhere.
All inputs are finite; a program needn't handle non-finite values.
Results may differ from a plain program's by a relative error of at most 0.0003.
Values sent between devices are 32-bit elements; how exact they have to be, the bound alone decides.
A program may use at most 128 MiB of HBM per device.

v0:
```python
import jax
import jax.numpy as jnp
from jax import lax
from jax.sharding import PartitionSpec as P


def swapped(x, axis, distance):
    return lax.ppermute(x, axis, [(i, i ^ 1 << distance) for i in range(lax.axis_size(axis))])


def sylvester(order):
    index = jnp.arange(order, dtype=jnp.int32)
    common = jnp.bitwise_and(index[:, None], index[None, :])
    parity = jnp.zeros((order, order), jnp.int32)
    for level in range(max(order.bit_length() - 1, 0)):
        parity = parity + jnp.bitwise_and(jnp.right_shift(common, level), 1)
    return (1 - 2 * (parity % 2)).astype(jnp.float32)


def body(panel, signs, offsets, owners):
    col_width, row_count = panel.shape
    devices = lax.axis_size("row")
    blocks = row_count // 128
    sample_count = offsets.shape[0]
    high = lax.Precision.HIGHEST
    scale = 1.0 / jnp.sqrt(jnp.float32(devices * row_count))
    signed = (panel * signs.astype(jnp.float32)[None, :]).reshape(col_width, 128, blocks)
    inner = jnp.einsum("cab,bd->cad", signed, sylvester(blocks), precision=high)
    mixed = jnp.einsum("ea,cad->ced", sylvester(128), inner, precision=high)
    mixed = mixed.reshape(col_width, row_count) * scale
    my_index = lax.axis_index("row")
    for level in range(devices.bit_length() - 1):
        partner = swapped(mixed, "row", level)
        upper = jnp.bitwise_and(jnp.right_shift(my_index, level), 1) == 1
        mixed = jnp.where(upper, partner - mixed, mixed + partner)
    sampled = jnp.take(mixed, offsets, axis=1)
    full_rows = lax.all_gather(sampled, "col", axis=0, tiled=True)
    total_cols = full_rows.shape[0]
    owner_ids = owners[:, 0]
    capacity = 2 * sample_count // devices
    hits = (owner_ids[:, None] == jnp.arange(devices, dtype=jnp.int32)[None, :]).astype(jnp.int32)
    before = jnp.cumsum(hits, axis=0) - hits
    slot_index = jnp.sum(before * hits, axis=1)
    position = owner_ids * capacity + slot_index
    buffer = jnp.zeros((total_cols, devices * capacity), jnp.float32).at[:, position].set(full_rows)
    received = lax.all_to_all(
        buffer.reshape(total_cols, devices, capacity),
        "row",
        split_axis=1,
        concat_axis=1,
        tiled=True,
    )
    received = received.reshape(total_cols, devices * capacity)
    mine = lax.dynamic_slice_in_dim(received, lax.axis_index("col") * col_width, col_width, 0)
    gram = jnp.einsum("ck,dk->cd", mine, received, precision=high) / sample_count
    return gram[None]


def solution(mesh):
    placed = (P("col", "row"), P("row"), P("row"), P("row", None))
    return jax.shard_map(
        body, mesh=mesh, in_specs=placed, out_specs=P("row", "col", None), check_vma=False
    )
```

profile of v0, /device:TPU:2, one launch (start us, length us, event | category | flops | bytes accessed | tf_op | source)
XLA Modules:
  0.0 333.8 jit_solution(12955752235051832701)
XLA Ops:
  0.0 0.8 convert_element_type.18
  0.8 1.3 multiply_bitcast_fusion
  2.2 0.2 copy.35
  2.4 1.1 fusion.15
  3.5 1.0 fusion
  4.6 0.3 copy.14
  4.9 0.6 copy.39
  5.5 2.4 collective-permute-start
  7.9 4.6 %copy.16 = f32[16,16384]{0,1:T(8,128)} copy(f32[16,16384]{1,0:T(8,128)S(1)} %bitcast.46) | data formatting | bytes 2097152 | tf_op jit(solution)/shard_map/mul | solution.py:30
  12.5 18.0 %collective-permute-done = f32[16,16384]{1,0:T(8,128)S(1)} collective-permute-done((f32[16,16384]{1,0:T(8,128)S(1)}, f32[16,16384]{1,0:T(8,128)S(1)}, u32[]{:S(2)}, u32[]{:S(2)}) %collective-permute-start) | collective-permute-done | bytes 1048608 | tf_op jit(solution)/shard_map/ppermute | solution.py:8
  30.5 4.6 %copy.15 = f32[16,16384]{0,1:T(8,128)} copy(f32[16,16384]{1,0:T(8,128)S(1)} %collective-permute-done) | data formatting | bytes 2097152 | tf_op jit(solution)/shard_map/ppermute | solution.py:8
  35.1 9.8 %add_select_fusion.4 = f32[16,16384]{0,1:T(8,128)} fusion(f32[16,16384]{0,1:T(8,128)} %copy.16, f32[16,16384]{0,1:T(8,128)} %copy.15, pred[]{:T(512)S(6)} %eq.55), kind=kLoop, calls=%fused_computation.6 | loop fusion | flops 786432 | bytes 3145729 | tf_op jit(solution)/shard_map/jit(_where)/select_n | solution.py:35
  44.9 5.1 %copy.19 = f32[16,16384]{1,0:T(8,128)S(1)} copy(f32[16,16384]{0,1:T(8,128)} %add_select_fusion.4) | data formatting | bytes 2097152 | tf_op jit(solution)/shard_map/jit(_where)/select_n | solution.py:35
  50.0 2.2 collective-permute-start.1
  52.2 23.1 %collective-permute-done.1 = f32[16,16384]{1,0:T(8,128)S(1)} collective-permute-done((f32[16,16384]{1,0:T(8,128)S(1)}, f32[16,16384]{1,0:T(8,128)S(1)}, u32[]{:S(2)}, u32[]{:S(2)}) %collective-permute-start.1) | collective-permute-done | bytes 1048608 | tf_op jit(solution)/shard_map/ppermute | solution.py:8
  75.3 4.6 %copy.20 = f32[16,16384]{0,1:T(8,128)} copy(f32[16,16384]{1,0:T(8,128)S(1)} %collective-permute-done.1) | data formatting | bytes 2097152 | tf_op jit(solution)/shard_map/ppermute | solution.py:8
  79.9 9.8 %add_select_fusion.3 = f32[16,16384]{0,1:T(8,128)} fusion(f32[16,16384]{0,1:T(8,128)} %add_select_fusion.4, f32[16,16384]{0,1:T(8,128)} %copy.20, pred[]{:T(512)S(6)} %eq.54), kind=kLoop, calls=%fused_computation.5 | loop fusion | flops 786432 | bytes 3145729 | tf_op jit(solution)/shard_map/jit(_where)/select_n | solution.py:35
  89.7 5.1 %copy.22 = f32[16,16384]{1,0:T(8,128)S(1)} copy(f32[16,16384]{0,1:T(8,128)} %add_select_fusion.3) | data formatting | bytes 2097152 | tf_op jit(solution)/shard_map/jit(_where)/select_n | solution.py:35
  94.8 2.3 collective-permute-start.2
  97.1 21.4 %collective-permute-done.2 = f32[16,16384]{1,0:T(8,128)S(1)} collective-permute-done((f32[16,16384]{1,0:T(8,128)S(1)}, f32[16,16384]{1,0:T(8,128)S(1)}, u32[]{:S(2)}, u32[]{:S(2)}) %collective-permute-start.2) | collective-permute-done | bytes 1048608 | tf_op jit(solution)/shard_map/ppermute | solution.py:8
  118.5 4.6 %copy.23 = f32[16,16384]{0,1:T(8,128)} copy(f32[16,16384]{1,0:T(8,128)S(1)} %collective-permute-done.2) | data formatting | bytes 2097152 | tf_op jit(solution)/shard_map/ppermute | solution.py:8
  123.1 9.8 %add_select_fusion.2 = f32[16,16384]{0,1:T(8,128)} fusion(f32[16,16384]{0,1:T(8,128)} %add_select_fusion.3, f32[16,16384]{0,1:T(8,128)} %copy.23, pred[]{:T(512)S(6)} %eq.53), kind=kLoop, calls=%fused_computation.4 | loop fusion | flops 786432 | bytes 3145729 | tf_op jit(solution)/shard_map/jit(_where)/select_n | solution.py:35
  132.8 5.1 %copy.25 = f32[16,16384]{1,0:T(8,128)S(1)} copy(f32[16,16384]{0,1:T(8,128)} %add_select_fusion.2) | data formatting | bytes 2097152 | tf_op jit(solution)/shard_map/jit(_where)/select_n | solution.py:35
  137.9 3.3 %collective-permute-start.3 = (f32[16,16384]{1,0:T(8,128)S(1)}, f32[16,16384]{1,0:T(8,128)S(1)}, u32[]{:S(2)}, u32[]{:S(2)}) collective-permute-start(f32[16,16384]{1,0:T(8,128)S(1)} %copy.25), channel_id=1, source_target_pairs={{0,64},{8,72},{16,80},{24,88},{32,96},{40,104},{48,112},{56,120},{... | collective-permute-start | bytes 3145736 | tf_op jit(solution)/shard_map/ppermute | solution.py:8
  141.3 43.1 %collective-permute-done.3 = f32[16,16384]{1,0:T(8,128)S(1)} collective-permute-done((f32[16,16384]{1,0:T(8,128)S(1)}, f32[16,16384]{1,0:T(8,128)S(1)}, u32[]{:S(2)}, u32[]{:S(2)}) %collective-permute-start.3) | collective-permute-done | bytes 1048608 | tf_op jit(solution)/shard_map/ppermute | solution.py:8
  184.4 4.6 %copy.26 = f32[16,16384]{0,1:T(8,128)} copy(f32[16,16384]{1,0:T(8,128)S(1)} %collective-permute-done.3) | data formatting | bytes 2097152 | tf_op jit(solution)/shard_map/ppermute | solution.py:8
  189.0 9.8 %add_select_fusion.1 = f32[16,16384]{0,1:T(8,128)} fusion(f32[16,16384]{0,1:T(8,128)} %add_select_fusion.2, f32[16,16384]{0,1:T(8,128)} %copy.26, pred[]{:T(512)S(6)} %eq.52), kind=kLoop, calls=%fused_computation.3 | loop fusion | flops 786432 | bytes 3145729 | tf_op jit(solution)/shard_map/jit(_where)/select_n | solution.py:35
  198.7 5.1 %copy.28 = f32[16,16384]{1,0:T(8,128)S(1)} copy(f32[16,16384]{0,1:T(8,128)} %add_select_fusion.1) | data formatting | bytes 2097152 | tf_op jit(solution)/shard_map/jit(_where)/select_n | solution.py:35
  203.9 6.5 %collective-permute-start.4 = (f32[16,16384]{1,0:T(8,128)S(1)}, f32[16,16384]{1,0:T(8,128)S(1)}, u32[]{:S(2)}, u32[]{:S(2)}) collective-permute-start(f32[16,16384]{1,0:T(8,128)S(1)} %copy.28), channel_id=1, source_target_pairs={{0,128},{8,136},{16,144},{24,152},{32,160},{40,168},{48,176},{56,1... | collective-permute-start | bytes 3145736 | tf_op jit(solution)/shard_map/ppermute | solution.py:8
  210.4 0.0 copy-done
  210.4 9.0 %reduce-window.6 = s32[32,8,128]{2,1,0:T(8,128)S(1)} reduce-window(s32[32,8,128]{2,1,0:T(8,128)S(1)} %fusion.8, s32[]{:T(128)} %constant.29.clone.1), window={size=1x1x128 pad=0_0x0_0x127_0}, to_apply=%region_0.1 | reduce-window | flops 4161536 | bytes 262148 | tf_op jit(solution)/shard_map/reduce-window
  219.4 0.1 slice.10
  219.5 0.1 copy.11
  219.7 0.1 copy.12
  219.8 0.1 broadcast_add_fusion
  219.9 0.0 copy-done.1
  220.0 36.2 %collective-permute-done.4 = f32[16,16384]{1,0:T(8,128)S(1)} collective-permute-done((f32[16,16384]{1,0:T(8,128)S(1)}, f32[16,16384]{1,0:T(8,128)S(1)}, u32[]{:S(2)}, u32[]{:S(2)}) %collective-permute-start.4) | collective-permute-done | bytes 1048608 | tf_op jit(solution)/shard_map/ppermute | solution.py:8
  256.1 4.6 %copy.29 = f32[16,16384]{0,1:T(8,128)} copy(f32[16,16384]{1,0:T(8,128)S(1)} %collective-permute-done.4) | data formatting | bytes 2097152 | tf_op jit(solution)/shard_map/ppermute | solution.py:8
  260.7 9.8 %add_select_fusion = f32[16,16384]{0,1:T(8,128)} fusion(f32[16,16384]{0,1:T(8,128)} %add_select_fusion.1, f32[16,16384]{0,1:T(8,128)} %copy.29, pred[]{:T(512)S(6)} %eq.51), kind=kLoop, calls=%fused_computation.2 | loop fusion | flops 786432 | bytes 3145729 | tf_op jit(solution)/shard_map/jit(_where)/select_n | solution.py:35
  270.5 6.2 %gather_fusion = f32[1024,16]{1,0:T(8,128)S(1)} fusion(f32[16,16384]{0,1:T(8,128)} %add_select_fusion, s32[1024]{0:T(1024)S(1)} %fusion.31), kind=kCustom, calls=%fused_computation | custom fusion | bytes 135168 | tf_op jit(solution)/shard_map/jit(_take)/gather | solution.py:36
  276.7 0.2 select_bitcast_fusion
  276.9 0.2 copy.31
  277.1 13.6 %all_gather.3 = f32[128,1024]{1,0:T(8,128)S(1)} all-gather(f32[16,1024]{1,0:T(8,128)S(1)} %copy.31), channel_id=1, replica_groups=mesh['row'=32,'col'=8] {'col'}, dimensions={0}, use_global_device_ids=true | all-gather | bytes 589824 | tf_op jit(solution)/shard_map/all_gather | solution.py:37
  290.6 0.2 copy.32
  290.8 4.1 %scatter_custom_fusion = f32[128,2048]{0,1:T(8,128)} fusion(s32[1024]{0:T(1024)S(1)} %bitcast.56, f32[1024,128]{1,0:T(8,128)S(1)} %copy.32, f32[]{:T(128)} %constant.24.clone.1), kind=kCustom, calls=%fused_computation.15 | custom fusion | bytes 1048580 | tf_op jit(solution)/shard_map/scatter | solution.py:45
  294.9 7.5 %all-to-all-start = ((f32[128,32,64]{0,2,1:T(8,128)}), f32[128,32,64]{0,2,1:T(8,128)S(1)}, u32[]{:S(2)}, u32[]{:S(2)}) async-start(f32[128,32,64]{0,2,1:T(8,128)} %bitcast.10), calls=%async_computation | async-start | bytes 2097152 | tf_op jit(solution)/shard_map/all_to_all | solution.py:46
  302.5 28.6 %all-to-all-done = f32[128,32,64]{0,2,1:T(8,128)S(1)} async-done(((f32[128,32,64]{0,2,1:T(8,128)}), f32[128,32,64]{0,2,1:T(8,128)S(1)}, u32[]{:S(2)}, u32[]{:S(2)}) %all-to-all-start) | async-done | bytes 1048608 | tf_op jit(solution)/shard_map/all_to_all | solution.py:46
  331.0 2.8 fusion.1
  (9 shorter events, 0.1 us)
Async XLA Ops:
  5.5 25.0 %collective-permute-start = (f32[16,16384]{1,0:T(8,128)S(1)}, f32[16,16384]{1,0:T(8,128)S(1)}, u32[]{:S(2)}, u32[]{:S(2)}) collective-permute-start(f32[16,16384]{1,0:T(8,128)S(1)} %bitcast.45), channel_id=1, source_target_pairs={{0,8},{8,0},{16,24},{24,16},{32,40},{40,32},{48,56},{56,48},{64,72... | collective-permute-start | bytes 3145736 | tf_op jit(solution)/shard_map/ppermute | solution.py:8
  50.0 25.3 %collective-permute-start.1 = (f32[16,16384]{1,0:T(8,128)S(1)}, f32[16,16384]{1,0:T(8,128)S(1)}, u32[]{:S(2)}, u32[]{:S(2)}) collective-permute-start(f32[16,16384]{1,0:T(8,128)S(1)} %copy.19), channel_id=1, source_target_pairs={{0,16},{8,24},{16,0},{24,8},{32,48},{40,56},{48,32},{56,40},{64,80... | collective-permute-start | bytes 3145736 | tf_op jit(solution)/shard_map/ppermute | solution.py:8
  94.8 23.7 %collective-permute-start.2 = (f32[16,16384]{1,0:T(8,128)S(1)}, f32[16,16384]{1,0:T(8,128)S(1)}, u32[]{:S(2)}, u32[]{:S(2)}) collective-permute-start(f32[16,16384]{1,0:T(8,128)S(1)} %copy.22), channel_id=1, source_target_pairs={{0,32},{8,40},{16,48},{24,56},{32,0},{40,8},{48,16},{56,24},{64,96... | collective-permute-start | bytes 3145736 | tf_op jit(solution)/shard_map/ppermute | solution.py:8
  137.9 46.4 %collective-permute-start.3 = (f32[16,16384]{1,0:T(8,128)S(1)}, f32[16,16384]{1,0:T(8,128)S(1)}, u32[]{:S(2)}, u32[]{:S(2)}) collective-permute-start(f32[16,16384]{1,0:T(8,128)S(1)} %copy.25), channel_id=1, source_target_pairs={{0,64},{8,72},{16,80},{24,88},{32,96},{40,104},{48,112},{56,120},{... | collective-permute-start | bytes 3145736 | tf_op jit(solution)/shard_map/ppermute | solution.py:8
  198.7 11.6 %copy-start = (s32[1024,1]{0,1:T(1,128)S(1)}, s32[1024,1]{0,1:T(1,128)}, u32[]{:S(2)}) copy-start(s32[1024,1]{0,1:T(1,128)} %param.7) | copy-start | bytes 12292
  198.7 21.2 %copy-start.1 = (s32[1024]{0:T(1024)S(1)}, s32[1024]{0:T(1024)}, u32[]{:S(2)}) copy-start(s32[1024]{0:T(1024)} %param.6) | copy-start | bytes 12292
  203.9 52.3 %collective-permute-start.4 = (f32[16,16384]{1,0:T(8,128)S(1)}, f32[16,16384]{1,0:T(8,128)S(1)}, u32[]{:S(2)}, u32[]{:S(2)}) collective-permute-start(f32[16,16384]{1,0:T(8,128)S(1)} %copy.28), channel_id=1, source_target_pairs={{0,128},{8,136},{16,144},{24,152},{32,160},{40,168},{48,176},{56,1... | collective-permute-start | bytes 3145736 | tf_op jit(solution)/shard_map/ppermute | solution.py:8
  294.9 36.1 %all-to-all-start = ((f32[128,32,64]{0,2,1:T(8,128)}), f32[128,32,64]{0,2,1:T(8,128)S(1)}, u32[]{:S(2)}, u32[]{:S(2)}) async-start(f32[128,32,64]{0,2,1:T(8,128)} %bitcast.10), calls=%async_computation | async-start | bytes 2097152 | tf_op jit(solution)/shard_map/all_to_all | solution.py:46
where the time goes:
time: 334 us
  waiting for transfers between devices  170 us (51%)
  other arithmetic  60.4 us (18%)
  local copies, waits for them, and re-layouts  60.2 us (18%)
  starting transfers between devices  24.2 us (7%)
  blocking collectives  13.6 us (4%)
  matrix products  4.97 us (1%)
    ppermute x5, waiting for transfers between devices, swapped(): lax.ppermute(x, axis, [(i, i ^ 1 << distance) for i in range(lax.axis_siz...  142 us
    select_n x5, other arithmetic, body(): mixed = jnp.where(upper, partner - mixed, mixed + partner)  48.8 us
    all_to_all x1, waiting for transfers between devices, body(): lax.all_to_all(buffer.reshape(total_cols, devices, capacity), 'row', spli...  28.6 us
    ppermute x5, local copies, waits for them, and re-layouts, swapped(): lax.ppermute(x, axis, [(i, i ^ 1 << distance) for i in range(lax.axis_siz...  23 us
    select_n x4, local copies, waits for them, and re-layouts, body(): mixed = jnp.where(upper, partner - mixed, mixed + partner)  20.5 us
    ppermute x5, starting transfers between devices, swapped(): lax.ppermute(x, axis, [(i, i ^ 1 << distance) for i in range(lax.axis_siz...  16.7 us
    all_gather x1, blocking collectives, body(): full_rows = lax.all_gather(sampled, 'col', axis=0, tiled=True)  13.6 us
    another operation x3, other arithmetic  9.15 us
  transfers between devices with their start and end apart: 6, of which 6 were waited for; matrix products, arithmetic and copies ran while one was open for 4% of the time, Pallas kernels for 0%

commit v1 on v0

--- a/solution.py
+++ b/solution.py
@@ -34,7 +34,24 @@
         upper = jnp.bitwise_and(jnp.right_shift(my_index, level), 1) == 1
         mixed = jnp.where(upper, partner - mixed, mixed + partner)
     sampled = jnp.take(mixed, offsets, axis=1)
-    full_rows = lax.all_gather(sampled, "col", axis=0, tiled=True)
+    peers, index_2, extent = (lax.axis_size("col"), lax.axis_index("col"), sampled.shape[0])
+    right = [(i_2, (i_2 + 1) % peers) for i_2 in range(peers)]
+    behind = [(i_2, (i_2 - 1) % peers) for i_2 in range(peers)]
+    out = jnp.zeros((*sampled.shape[:0], peers * extent, *sampled.shape[0 + 1 :]), sampled.dtype)
+    out = lax.dynamic_update_slice_in_dim(out, sampled, index_2 * extent, axis=0)
+    from_left = from_right = sampled
+    half = peers // 2
+    for step in range(1, half + 1):
+        from_left = lax.ppermute(from_left, "col", right)
+        out = lax.dynamic_update_slice_in_dim(
+            out, from_left, (index_2 - step) % peers * extent, axis=0
+        )
+        if step < peers - half:
+            from_right = lax.ppermute(from_right, "col", behind)
+            out = lax.dynamic_update_slice_in_dim(
+                out, from_right, (index_2 + step) % peers * extent, axis=0
+            )
+    full_rows = out
     total_cols = full_rows.shape[0]
     owner_ids = owners[:, 0]
     capacity = 2 * sample_count // devices

time: 334 us -> 378 us (1.13)
  local copies, waits for them, and re-layouts: 60.2 us -> 87 us
  blocking collectives: 13.6 us -> 34 us
  waiting for transfers between devices: 170 us -> 165 us
    all_to_all x0 -> x1, blocking collectives: none -> 34 us  [body(): lax.all_to_all(buffer.reshape(total_cols, devices, capacity), 'row', spli...]
    all_to_all x1 -> x0, waiting for transfers between devices: 28.6 us -> none  [body(): lax.all_to_all(buffer.reshape(total_cols, devices, capacity), 'row', spli...]
    dynamic_update_slice x0 -> x8, local copies, waits for them, and re-layouts: none -> 28 us  [the longest x4 13.7 us: body(): lax.dynamic_update_slice_in_dim(out, from_left, (index_2 - step) % peers...]
    all_gather x1 -> x0, blocking collectives: 13.6 us -> none  [body(): full_rows = lax.all_gather(sampled, 'col', axis=0, tiled=True)]
    ppermute x0 -> x7, waiting for transfers between devices: none -> 13.3 us  [the longest x3 13.2 us: body(): from_right = lax.ppermute(from_right, 'col', behind)]
    ppermute x5, waiting for transfers between devices: 142 us -> 151 us  [swapped(): lax.ppermute(x, axis, [(i, i ^ 1 << distance) for i in range(lax.axis_siz...]
    ppermute x0 -> x7, starting transfers between devices: none -> 9.3 us  [the longest x3 9.28 us: body(): from_right = lax.ppermute(from_right, 'col', behind)]
    all_to_all x1 -> x0, starting transfers between devices: 7.51 us -> none  [body(): lax.all_to_all(buffer.reshape(total_cols, devices, capacity), 'row', spli...]
  transfers between devices with their start and end apart: 6 -> 12, of which waited for: 6 -> 7; matrix products, arithmetic and copies ran while one was open for 4% -> 10% of each run, Pallas kernels for 0% -> 0%
where the time goes in v1:
time: 378 us; the launch traced here: 377 us
  waiting for transfers between devices  165 us (44%)
  local copies, waits for them, and re-layouts  87 us (23%)
  other arithmetic  60.3 us (16%)
  blocking collectives  34 us (9%)
  starting transfers between devices  26 us (7%)
  matrix products  4.97 us (1%)
    ppermute x5, waiting for transfers between devices, swapped(): lax.ppermute(x, axis, [(i, i ^ 1 << distance) for i in range(lax.axis_siz...  151 us
    select_n x5, other arithmetic, body(): mixed = jnp.where(upper, partner - mixed, mixed + partner)  48.7 us
    all_to_all x1, blocking collectives, body(): lax.all_to_all(buffer.reshape(total_cols, devices, capacity), 'row', spli...  34 us
    ppermute x5, local copies, waits for them, and re-layouts, swapped(): lax.ppermute(x, axis, [(i, i ^ 1 << distance) for i in range(lax.axis_siz...  22.9 us
    select_n x4, local copies, waits for them, and re-layouts, body(): mixed = jnp.where(upper, partner - mixed, mixed + partner)  20.4 us
    ppermute x5, starting transfers between devices, swapped(): lax.ppermute(x, axis, [(i, i ^ 1 << distance) for i in range(lax.axis_siz...  16.7 us
    dynamic_update_slice x4, local copies, waits for them, and re-layouts, body(): lax.dynamic_update_slice_in_dim(out, from_left, (index_2 - step) % peers...  13.7 us
    ppermute x3, waiting for transfers between devices, body(): from_right = lax.ppermute(from_right, 'col', behind)  13.2 us
  transfers between devices with their start and end apart: 12, of which 7 were waited for; matrix products, arithmetic and copies ran while one was open for 10% of the time, Pallas kernels for 0%

profile of v1, /device:TPU:2, one launch (start us, length us, event | category | flops | bytes accessed | tf_op | source)
XLA Modules:
  0.0 377.3 jit_solution(15505392564032501810)
XLA Ops:
  0.0 0.8 convert_element_type.18
  0.8 1.3 multiply_bitcast_fusion
  2.4 1.1 fusion.16
  3.5 1.0 fusion
  4.9 0.6 copy.37
  5.5 2.4 collective-permute-start
  7.9 4.6 %copy.16 = f32[16,16384]{0,1:T(8,128)} copy(f32[16,16384]{1,0:T(8,128)S(1)} %bitcast.48) | data formatting | bytes 2097152 | tf_op jit(solution)/shard_map/mul | solution.py:30
  12.5 18.0 %collective-permute-done = f32[16,16384]{1,0:T(8,128)S(1)} collective-permute-done((f32[16,16384]{1,0:T(8,128)S(1)}, f32[16,16384]{1,0:T(8,128)S(1)}, u32[]{:S(2)}, u32[]{:S(2)}) %collective-permute-start) | collective-permute-done | bytes 1048608 | tf_op jit(solution)/shard_map/ppermute | solution.py:8
  30.5 4.6 %copy.15 = f32[16,16384]{0,1:T(8,128)} copy(f32[16,16384]{1,0:T(8,128)S(1)} %collective-permute-done) | data formatting | bytes 2097152 | tf_op jit(solution)/shard_map/ppermute | solution.py:8
  35.1 9.7 %add_select_fusion.4 = f32[16,16384]{0,1:T(8,128)} fusion(f32[16,16384]{0,1:T(8,128)} %copy.16, f32[16,16384]{0,1:T(8,128)} %copy.15, pred[]{:T(512)S(6)} %eq.63), kind=kLoop, calls=%fused_computation.6 | loop fusion | flops 786432 | bytes 3145729 | tf_op jit(solution)/shard_map/jit(_where)/select_n | solution.py:35
  44.8 5.1 %copy.19 = f32[16,16384]{1,0:T(8,128)S(1)} copy(f32[16,16384]{0,1:T(8,128)} %add_select_fusion.4) | data formatting | bytes 2097152 | tf_op jit(solution)/shard_map/jit(_where)/select_n | solution.py:35
  50.0 2.2 collective-permute-start.1
  52.2 23.1 %collective-permute-done.1 = f32[16,16384]{1,0:T(8,128)S(1)} collective-permute-done((f32[16,16384]{1,0:T(8,128)S(1)}, f32[16,16384]{1,0:T(8,128)S(1)}, u32[]{:S(2)}, u32[]{:S(2)}) %collective-permute-start.1) | collective-permute-done | bytes 1048608 | tf_op jit(solution)/shard_map/ppermute | solution.py:8
  75.3 4.6 %copy.20 = f32[16,16384]{0,1:T(8,128)} copy(f32[16,16384]{1,0:T(8,128)S(1)} %collective-permute-done.1) | data formatting | bytes 2097152 | tf_op jit(solution)/shard_map/ppermute | solution.py:8
  79.9 9.7 %add_select_fusion.3 = f32[16,16384]{0,1:T(8,128)} fusion(f32[16,16384]{0,1:T(8,128)} %add_select_fusion.4, f32[16,16384]{0,1:T(8,128)} %copy.20, pred[]{:T(512)S(6)} %eq.62), kind=kLoop, calls=%fused_computation.5 | loop fusion | flops 786432 | bytes 3145729 | tf_op jit(solution)/shard_map/jit(_where)/select_n | solution.py:35
  89.6 5.1 %copy.22 = f32[16,16384]{1,0:T(8,128)S(1)} copy(f32[16,16384]{0,1:T(8,128)} %add_select_fusion.3) | data formatting | bytes 2097152 | tf_op jit(solution)/shard_map/jit(_where)/select_n | solution.py:35
  94.7 2.3 collective-permute-start.2
  97.0 21.4 %collective-permute-done.2 = f32[16,16384]{1,0:T(8,128)S(1)} collective-permute-done((f32[16,16384]{1,0:T(8,128)S(1)}, f32[16,16384]{1,0:T(8,128)S(1)}, u32[]{:S(2)}, u32[]{:S(2)}) %collective-permute-start.2) | collective-permute-done | bytes 1048608 | tf_op jit(solution)/shard_map/ppermute | solution.py:8
  118.4 4.6 %copy.23 = f32[16,16384]{0,1:T(8,128)} copy(f32[16,16384]{1,0:T(8,128)S(1)} %collective-permute-done.2) | data formatting | bytes 2097152 | tf_op jit(solution)/shard_map/ppermute | solution.py:8
  123.0 9.7 %add_select_fusion.2 = f32[16,16384]{0,1:T(8,128)} fusion(f32[16,16384]{0,1:T(8,128)} %add_select_fusion.3, f32[16,16384]{0,1:T(8,128)} %copy.23, pred[]{:T(512)S(6)} %eq.61), kind=kLoop, calls=%fused_computation.4 | loop fusion | flops 786432 | bytes 3145729 | tf_op jit(solution)/shard_map/jit(_where)/select_n | solution.py:35
  132.7 5.1 %copy.25 = f32[16,16384]{1,0:T(8,128)S(1)} copy(f32[16,16384]{0,1:T(8,128)} %add_select_fusion.2) | data formatting | bytes 2097152 | tf_op jit(solution)/shard_map/jit(_where)/select_n | solution.py:35
  137.8 3.3 collective-permute-start.3
  141.2 43.1 %collective-permute-done.3 = f32[16,16384]{1,0:T(8,128)S(1)} collective-permute-done((f32[16,16384]{1,0:T(8,128)S(1)}, f32[16,16384]{1,0:T(8,128)S(1)}, u32[]{:S(2)}, u32[]{:S(2)}) %collective-permute-start.3) | collective-permute-done | bytes 1048608 | tf_op jit(solution)/shard_map/ppermute | solution.py:8
  184.2 4.6 %copy.26 = f32[16,16384]{0,1:T(8,128)} copy(f32[16,16384]{1,0:T(8,128)S(1)} %collective-permute-done.3) | data formatting | bytes 2097152 | tf_op jit(solution)/shard_map/ppermute | solution.py:8
  188.8 9.7 %add_select_fusion.1 = f32[16,16384]{0,1:T(8,128)} fusion(f32[16,16384]{0,1:T(8,128)} %add_select_fusion.2, f32[16,16384]{0,1:T(8,128)} %copy.26, pred[]{:T(512)S(6)} %eq.60), kind=kLoop, calls=%fused_computation.3 | loop fusion | flops 786432 | bytes 3145729 | tf_op jit(solution)/shard_map/jit(_where)/select_n | solution.py:35
  198.6 5.1 %copy.28 = f32[16,16384]{1,0:T(8,128)S(1)} copy(f32[16,16384]{0,1:T(8,128)} %add_select_fusion.1) | data formatting | bytes 2097152 | tf_op jit(solution)/shard_map/jit(_where)/select_n | solution.py:35
  203.7 6.5 %collective-permute-start.4 = (f32[16,16384]{1,0:T(8,128)S(1)}, f32[16,16384]{1,0:T(8,128)S(1)}, u32[]{:S(2)}, u32[]{:S(2)}) collective-permute-start(f32[16,16384]{1,0:T(8,128)S(1)} %copy.28), channel_id=1, source_target_pairs={{0,128},{8,136},{16,144},{24,152},{32,160},{40,168},{48,176},{56,1... | collective-permute-start | bytes 3145736 | tf_op jit(solution)/shard_map/ppermute | solution.py:8
  210.2 45.7 %collective-permute-done.4 = f32[16,16384]{1,0:T(8,128)S(1)} collective-permute-done((f32[16,16384]{1,0:T(8,128)S(1)}, f32[16,16384]{1,0:T(8,128)S(1)}, u32[]{:S(2)}, u32[]{:S(2)}) %collective-permute-start.4) | collective-permute-done | bytes 1048608 | tf_op jit(solution)/shard_map/ppermute | solution.py:8
  256.0 4.6 %copy.29 = f32[16,16384]{0,1:T(8,128)} copy(f32[16,16384]{1,0:T(8,128)S(1)} %collective-permute-done.4) | data formatting | bytes 2097152 | tf_op jit(solution)/shard_map/ppermute | solution.py:8
  260.5 9.8 %add_select_fusion = f32[16,16384]{0,1:T(8,128)} fusion(f32[16,16384]{0,1:T(8,128)} %add_select_fusion.1, f32[16,16384]{0,1:T(8,128)} %copy.29, pred[]{:T(512)S(6)} %eq.59), kind=kLoop, calls=%fused_computation.2 | loop fusion | flops 786432 | bytes 3145729 | tf_op jit(solution)/shard_map/jit(_where)/select_n | solution.py:35
  270.3 6.2 %gather_fusion = f32[1024,16]{1,0:T(8,128)S(1)} fusion(f32[16,16384]{0,1:T(8,128)} %add_select_fusion, s32[1024]{0:T(1024)S(1)} %fusion.32), kind=kCustom, calls=%fused_computation | custom fusion | bytes 135168 | tf_op jit(solution)/shard_map/jit(_take)/gather | solution.py:36
  276.8 9.0 %reduce-window.6 = s32[32,8,128]{2,1,0:T(8,128)S(1)} reduce-window(s32[32,8,128]{2,1,0:T(8,128)S(1)} %fusion.9, s32[]{:T(128)} %constant.98.clone.1), window={size=1x1x128 pad=0_0x0_0x127_0}, to_apply=%region_0.1 | reduce-window | flops 4161536 | bytes 262148 | tf_op jit(solution)/shard_map/reduce-window
  286.1 2.9 collective-permute-start.6
  289.2 6.6 %collective-permute-done.6 = f32[16,1024]{0,1:T(8,128)S(1)} collective-permute-done((f32[16,1024]{0,1:T(8,128)S(1)}, f32[16,1024]{0,1:T(8,128)S(1)}, u32[]{:S(2)}, u32[]{:S(2)}) %collective-permute-start.6) | collective-permute-done | bytes 65568 | tf_op jit(solution)/shard_map/ppermute | solution.py:50
  295.8 3.1 collective-permute-start.8
  298.9 6.6 %collective-permute-done.8 = f32[16,1024]{0,1:T(8,128)} collective-permute-done((f32[16,1024]{0,1:T(8,128)S(1)}, f32[16,1024]{0,1:T(8,128)}, u32[]{:S(2)}, u32[]{:S(2)}) %collective-permute-start.8) | collective-permute-done | bytes 65568 | tf_op jit(solution)/shard_map/ppermute | solution.py:50
  305.6 3.2 collective-permute-start.10
  309.0 2.3 dynamic_update_slice.24
  311.3 3.1 dynamic_update_slice.25
  314.4 3.1 dynamic_update_slice.26
  317.4 3.1 dynamic_update_slice.27
  320.5 4.5 %dynamic_update_slice.28 = f32[128,1024]{0,1:T(8,128)S(1)} dynamic-update-slice(f32[128,1024]{0,1:T(8,128)S(1)} %dynamic_update_slice.27, f32[16,1024]{0,1:T(8,128)} %collective-permute-done.8, s32[]{:T(128)S(6)} %select_n.133, s32[]{:T(128)} %constant.98.clone.1) | dynamic-update-slice | bytes 131076 | tf_op jit(solution)/shard_map/dynamic_update_slice | solution.py:51
  325.0 3.1 dynamic_update_slice.29
  328.1 4.5 %dynamic_update_slice.30 = f32[128,1024]{0,1:T(8,128)S(1)} dynamic-update-slice(f32[128,1024]{0,1:T(8,128)S(1)} %dynamic_update_slice.29, f32[16,1024]{0,1:T(8,128)} %collective-permute-done.10, s32[]{:T(128)S(6)} %select_n.137, s32[]{:T(128)} %constant.98.clone.1) | dynamic-update-slice | bytes 131076 | tf_op jit(solution)/shard_map/dynamic_update_slice | solution.py:51
  332.6 4.5 %dynamic_update_slice.31 = f32[128,1024]{0,1:T(8,128)S(1)} dynamic-update-slice(f32[128,1024]{0,1:T(8,128)S(1)} %dynamic_update_slice.30, f32[16,1024]{0,1:T(8,128)} %collective-permute-done.11, s32[]{:T(128)S(6)} %select_n.139, s32[]{:T(128)} %constant.98.clone.1) | dynamic-update-slice | bytes 131076 | tf_op jit(solution)/shard_map/dynamic_update_slice | solution.py:46
  337.1 3.4 scatter_custom_fusion
  340.5 34.0 %all_to_all.5 = f32[128,32,64]{0,2,1:T(8,128)S(1)} all-to-all(f32[128,32,64]{0,2,1:T(8,128)S(1)} %bitcast.49), channel_id=1, replica_groups=mesh['row'=32,'col'=8] {'row'}, dimensions={1} | all-to-all | bytes 2097152 | tf_op jit(solution)/shard_map/all_to_all | solution.py:63
  374.5 2.8 fusion.1
  (28 shorter events, 1.3 us)
Async XLA Ops:
  5.5 25.0 %collective-permute-start = (f32[16,16384]{1,0:T(8,128)S(1)}, f32[16,16384]{1,0:T(8,128)S(1)}, u32[]{:S(2)}, u32[]{:S(2)}) collective-permute-start(f32[16,16384]{1,0:T(8,128)S(1)} %bitcast.47), channel_id=1, source_target_pairs={{0,8},{8,0},{16,24},{24,16},{32,40},{40,32},{48,56},{56,48},{64,72... | collective-permute-start | bytes 3145736 | tf_op jit(solution)/shard_map/ppermute | solution.py:8
  50.0 25.3 %collective-permute-start.1 = (f32[16,16384]{1,0:T(8,128)S(1)}, f32[16,16384]{1,0:T(8,128)S(1)}, u32[]{:S(2)}, u32[]{:S(2)}) collective-permute-start(f32[16,16384]{1,0:T(8,128)S(1)} %copy.19), channel_id=1, source_target_pairs={{0,16},{8,24},{16,0},{24,8},{32,48},{40,56},{48,32},{56,40},{64,80... | collective-permute-start | bytes 3145736 | tf_op jit(solution)/shard_map/ppermute | solution.py:8
  94.7 23.7 %collective-permute-start.2 = (f32[16,16384]{1,0:T(8,128)S(1)}, f32[16,16384]{1,0:T(8,128)S(1)}, u32[]{:S(2)}, u32[]{:S(2)}) collective-permute-start(f32[16,16384]{1,0:T(8,128)S(1)} %copy.22), channel_id=1, source_target_pairs={{0,32},{8,40},{16,48},{24,56},{32,0},{40,8},{48,16},{56,24},{64,96... | collective-permute-start | bytes 3145736 | tf_op jit(solution)/shard_map/ppermute | solution.py:8
  137.8 46.4 %collective-permute-start.3 = (f32[16,16384]{1,0:T(8,128)S(1)}, f32[16,16384]{1,0:T(8,128)S(1)}, u32[]{:S(2)}, u32[]{:S(2)}) collective-permute-start(f32[16,16384]{1,0:T(8,128)S(1)} %copy.25), channel_id=1, source_target_pairs={{0,64},{8,72},{16,80},{24,88},{32,96},{40,104},{48,112},{56,120},{... | collective-permute-start | bytes 3145736 | tf_op jit(solution)/shard_map/ppermute | solution.py:8
  198.6 11.6 %copy-start.1 = (s32[1024]{0:T(1024)S(1)}, s32[1024]{0:T(1024)}, u32[]{:S(2)}) copy-start(s32[1024]{0:T(1024)} %param.6) | copy-start | bytes 12292
  203.7 52.3 %collective-permute-start.4 = (f32[16,16384]{1,0:T(8,128)S(1)}, f32[16,16384]{1,0:T(8,128)S(1)}, u32[]{:S(2)}, u32[]{:S(2)}) collective-permute-start(f32[16,16384]{1,0:T(8,128)S(1)} %copy.28), channel_id=1, source_target_pairs={{0,128},{8,136},{16,144},{24,152},{32,160},{40,168},{48,176},{56,1... | collective-permute-start | bytes 3145736 | tf_op jit(solution)/shard_map/ppermute | solution.py:8
  260.5 16.2 %copy-start = (s32[1024,1]{0,1:T(1,128)S(1)}, s32[1024,1]{0,1:T(1,128)}, u32[]{:S(2)}) copy-start(s32[1024,1]{0,1:T(1,128)} %param.7) | copy-start | bytes 12292
  276.7 12.4 %collective-permute-start.5 = (f32[16,1024]{0,1:T(8,128)S(1)}, f32[16,1024]{0,1:T(8,128)S(1)}, u32[]{:S(2)}, u32[]{:S(2)}) collective-permute-start(f32[16,1024]{0,1:T(8,128)S(1)} %select_bitcast_fusion), channel_id=1, source_target_pairs={{0,1},{1,2},{2,3},{3,4},{4,5},{5,6},{6,7},{7,0},{8,9},{9,10},{10,1... | collective-permute-start | bytes 196616 | tf_op jit(solution)/shard_map/ppermute | solution.py:45
  286.1 9.6 %collective-permute-start.6 = (f32[16,1024]{0,1:T(8,128)S(1)}, f32[16,1024]{0,1:T(8,128)S(1)}, u32[]{:S(2)}, u32[]{:S(2)}) collective-permute-start(f32[16,1024]{0,1:T(8,128)S(1)} %select_bitcast_fusion), channel_id=1, source_target_pairs={{0,7},{1,0},{2,1},{3,2},{4,3},{5,4},{6,5},{7,6},{8,15},{9,8},{10,9... | collective-permute-start | bytes 196616 | tf_op jit(solution)/shard_map/ppermute | solution.py:50
  289.1 9.8 %collective-permute-start.7 = (f32[16,1024]{0,1:T(8,128)S(1)}, f32[16,1024]{0,1:T(8,128)S(1)}, u32[]{:S(2)}, u32[]{:S(2)}) collective-permute-start(f32[16,1024]{0,1:T(8,128)S(1)} %collective-permute-done.5), channel_id=1, source_target_pairs={{0,1},{1,2},{2,3},{3,4},{4,5},{5,6},{6,7},{7,0},{8,9},{9,10},{10,1... | collective-permute-start | bytes 196616 | tf_op jit(solution)/shard_map/ppermute | solution.py:45
  295.8 9.8 %collective-permute-start.8 = (f32[16,1024]{0,1:T(8,128)S(1)}, f32[16,1024]{0,1:T(8,128)}, u32[]{:S(2)}, u32[]{:S(2)}) collective-permute-start(f32[16,1024]{0,1:T(8,128)S(1)} %collective-permute-done.6), channel_id=1, source_target_pairs={{0,7},{1,0},{2,1},{3,2},{4,3},{5,4},{6,5},{7,6},{8,15},{9,8},{10,9... | collective-permute-start | bytes 196616 | tf_op jit(solution)/shard_map/ppermute | solution.py:50
  298.9 9.9 %collective-permute-start.9 = (f32[16,1024]{0,1:T(8,128)S(1)}, f32[16,1024]{0,1:T(8,128)S(1)}, u32[]{:S(2)}, u32[]{:S(2)}) collective-permute-start(f32[16,1024]{0,1:T(8,128)S(1)} %collective-permute-done.7), channel_id=1, source_target_pairs={{0,1},{1,2},{2,3},{3,4},{4,5},{5,6},{6,7},{7,0},{8,9},{9,10},{10,1... | collective-permute-start | bytes 196616 | tf_op jit(solution)/shard_map/ppermute | solution.py:45
  305.6 22.5 %collective-permute-start.10 = (f32[16,1024]{0,1:T(8,128)}, f32[16,1024]{0,1:T(8,128)}, u32[]{:S(2)}, u32[]{:S(2)}) collective-permute-start(f32[16,1024]{0,1:T(8,128)} %collective-permute-done.8), channel_id=1, source_target_pairs={{0,7},{1,0},{2,1},{3,2},{4,3},{5,4},{6,5},{7,6},{8,15},{9,8},{10,9... | collective-permute-start | bytes 196616 | tf_op jit(solution)/shard_map/ppermute | solution.py:50
  308.8 23.8 %collective-permute-start.11 = (f32[16,1024]{0,1:T(8,128)S(1)}, f32[16,1024]{0,1:T(8,128)}, u32[]{:S(2)}, u32[]{:S(2)}) collective-permute-start(f32[16,1024]{0,1:T(8,128)S(1)} %collective-permute-done.9), channel_id=1, source_target_pairs={{0,1},{1,2},{2,3},{3,4},{4,5},{5,6},{6,7},{7,0},{8,9},{9,10},{10,1... | collective-permute-start | bytes 196616 | tf_op jit(solution)/shard_map/ppermute | solution.py:45
